TPU v7x, 32 devices: a whole 2x2x4 slice. The times are simulated.
32 devices in a mesh: grp: 2 (over y), row: 16 (over z, x, core).
Axes of the slice: x: 2, y: 2, z: 4, core: 2. Of those that a mesh axis runs over, the one named last changes fastest.
Arguments:
- voltages: bfloat16 [256, 262144], P('grp', 'row'), parts along dimension 0, may hold values from -8 to 8
- taps: float32 [3, 8192], replicated, may hold values from -3 to 3
- station_order: int32 [128], P('grp'), parts along dimension 0, may hold values from 0 to 63, each once
- pair_list: int32 [16, 2], P('grp'), parts along dimension 0, may hold values from 0 to 3, as said below
Outputs:
- visibilities: float32 [2, 4096, 16, 1024], P(None, 'row', 'grp'), parts along dimension 2
There are 2 independent parts, one for each index of `grp`. A program takes and returns all parts, laid end to end along the dimension named above; an argument that names none is the same for every part. Nothing has to cross between parts.
Inputs may be any that keep to these rules, and one draw needn't show every extreme that they name: `station_order`: a permutation of the stations. `pair_list`: distinct pairs (first, second) of block numbers with first <= second, sorted by first and then second; the pair (0, 3) is always listed.
All inputs are finite; a program needn't handle non-finite values.
Results may differ from a plain program's by a relative error of at most 0.0022.
Values may be sent and summed in bfloat16 or wider, within the bound.
A program may use at most 320 MiB of HBM per device.

v0:
```python
import math

import jax
import jax.numpy as jnp
from jax import lax
from jax.sharding import PartitionSpec as P

BLOCK_SIZE = 32
DFT_OUTER = 64
DFT_INNER = 128


split_mode = lax.Precision.HIGH


def dft_tables(outer_len, inner_len):
    length_all = outer_len * inner_len
    inner_index = jnp.arange(inner_len, dtype=jnp.int32)
    outer_index = jnp.arange(outer_len, dtype=jnp.int32)
    half_index = jnp.arange(outer_len // 2, dtype=jnp.int32)
    first_angle = (
        2.0
        * math.pi
        / inner_len
        * (inner_index[:, None] * inner_index[None, :] % inner_len).astype(jnp.float32)
    )
    twist_angle = (
        2.0
        * math.pi
        / length_all
        * (outer_index[:, None] * inner_index[None, :]).astype(jnp.float32)
    )
    second_angle = (
        2.0
        * math.pi
        / outer_len
        * (outer_index[:, None] * half_index[None, :] % outer_len).astype(jnp.float32)
    )
    scaling = 1.0 / math.sqrt(length_all)
    first_table = jnp.concatenate([jnp.cos(first_angle), -jnp.sin(first_angle)], 1)
    second_cos = scaling * jnp.cos(second_angle)
    second_sin = scaling * jnp.sin(second_angle)
    second_table = jnp.stack(
        [jnp.stack([second_cos, -second_sin], 1), jnp.stack([second_sin, second_cos], 1)], 0
    )
    return (first_table, jnp.cos(twist_angle), jnp.sin(twist_angle), second_table)


def transform(filtered, tables, outer_len, inner_len):
    first_table, twist_cos, twist_sin, second_table = tables
    row_count = filtered.shape[0]
    folded = filtered.reshape(row_count, inner_len, outer_len)
    section = jnp.einsum("mbn,bq->mnq", folded, first_table, precision=split_mode)
    section = section.reshape(row_count, outer_len, 2, inner_len)
    section_real = section[:, :, 0]
    section_imag = section[:, :, 1]
    turned = jnp.stack(
        [
            section_real * twist_cos + section_imag * twist_sin,
            section_imag * twist_cos - section_real * twist_sin,
        ],
        0,
    )
    result = jnp.einsum("rmnk,rnqj->qjkm", turned, second_table, precision=split_mode)
    channel_count = outer_len // 2 * inner_len
    return result.reshape(2, channel_count, row_count).astype(jnp.bfloat16)


def input_order(station_order):
    station_count = station_order.shape[0]
    position = jnp.arange(2 * station_count, dtype=jnp.int32)
    return 2 * jnp.take(station_order, position // 2) + position % 2


def apply_filter(extended, taps, spectra_count):
    tap_count = taps.shape[0]
    filtered = taps[0][None, None, :] * extended[0:spectra_count].astype(jnp.float32)
    for tap_index in range(1, tap_count):
        filtered = filtered + taps[tap_index][None, None, :] * extended[
            tap_index : tap_index + spectra_count
        ].astype(jnp.float32)
    return filtered


def shards(voltages, taps, station_order, pair_list):
    tables = dft_tables(DFT_OUTER, DFT_INNER)
    tap_count, block_length = taps.shape
    order = input_order(station_order)
    owned_series = lax.all_to_all(voltages, "row", split_axis=0, concat_axis=1, tiled=True)
    input_count, sample_count = owned_series.shape
    spectra_count = sample_count // block_length
    series_blocks = jnp.transpose(
        owned_series.reshape(input_count, spectra_count, block_length), (1, 0, 2)
    )
    extended = jnp.concatenate(
        [jnp.zeros((tap_count - 1, input_count, block_length), jnp.bfloat16), series_blocks], 0
    )
    filtered = apply_filter(extended, taps, spectra_count)
    spectra_local = transform(
        filtered.reshape(spectra_count * input_count, block_length), tables, DFT_OUTER, DFT_INNER
    )
    spectra_local = spectra_local.reshape(2, -1, spectra_count, input_count)
    turned = lax.all_to_all(spectra_local, "row", split_axis=1, concat_axis=3, tiled=True)
    spectra_total = turned.shape[2]
    channel_count = turned.shape[1]
    ordered = jnp.take(turned, order, axis=3)
    block_count = ordered.shape[3] // BLOCK_SIZE
    tiled = ordered.reshape(2, channel_count, spectra_total, block_count, BLOCK_SIZE)
    left_blocks = jnp.take(tiled, pair_list[:, 0], axis=3)
    right_blocks = jnp.take(tiled, pair_list[:, 1], axis=3)

    def product(operand_one, operand_two):
        return jnp.einsum(
            "cspa,cspb->cpab", operand_one, operand_two, preferred_element_type=jnp.float32
        )

    vis_real = product(left_blocks[0], right_blocks[0]) + product(left_blocks[1], right_blocks[1])
    vis_imag = product(left_blocks[1], right_blocks[0]) - product(left_blocks[0], right_blocks[1])
    stacked = jnp.stack([vis_real, vis_imag]) * (1.0 / spectra_total)
    return stacked.reshape(2, stacked.shape[1], stacked.shape[2], -1)


def solution(mesh):
    placed = (P("grp", "row"), P(), P("grp"), P("grp", None))
    return jax.shard_map(
        shards, mesh=mesh, in_specs=placed, out_specs=P(None, "row", "grp", None), check_vma=False
    )
```

profile of v0, /device:TPU:11, one launch (start us, length us, event | category | flops | bytes accessed | tf_op | source)
XLA Modules:
  0.0 730.7 jit_solution(18440032069802170695)
XLA Ops:
  0.0 6.7 all-to-all-start
  8.5 90.6 %all-to-all-done = bf16[16,8,16384]{2,1,0:T(8,128)(2,1)} async-done(((bf16[16,8,16384]{2,1,0:T(8,128)(2,1)}), bf16[16,8,16384]{2,1,0:T(8,128)(2,1)}, u32[]{:S(2)}, u32[]{:S(2)}) %all-to-all-start) | async-done | bytes 4194336 | tf_op jit(solution)/shard_map/all_to_all | solution.py:89
  99.2 7.9 %multiply_add_fusion.1 = f32[32,8,8192]{2,1,0:T(8,128)} fusion(bf16[32,8,8192]{2,1,0:T(8,128)(2,1)} %bitcast.11, f32[8192]{0:T(1024)S(1)} %bitcast.121, f32[8192]{0:T(1024)S(1)} %bitcast.122, f32[8192]{0:T(1024)S(1)} %bitcast.120), kind=kLoop, calls=%fused_computation.26 | loop fusion | flops 16777216 | bytes 12681216 | tf_op jit(solution)/shard_map/add | solution.py:79
  107.1 14.2 %reshape_reshape.3 = f32[256,128,64]{2,1,0:T(8,128)} reshape(f32[32,8,8192]{2,1,0:T(8,128)} %multiply_add_fusion.1) | data formatting | bytes 16777216 | tf_op jit(solution)/shard_map/reshape;reshape | solution.py:52
  121.2 13.6 %copy.43 = f32[256,128,64,1]{1,0,3,2:T(8,128)} copy(f32[256,128,64,1]{2,1,0,3:T(8,128)} %bitcast.113) | data formatting | bytes 16777216 | tf_op jit(solution)/shard_map/reshape;reshape | solution.py:52
  134.8 9.1 %fusion.41 = f32[256,64,2,128]{3,0,2,1:T(8,128)S(1)} fusion(f32[256,128,64,1]{1,0,3,2:T(8,128)} %copy.43, f32[2,128,128,1]{2,1,0,3:T(8,128)S(1)} %bitcast.119), kind=kOutput, calls=%fused_computation.95 | convolution fusion | flops 3221225472 | bytes 25296896 | tf_op jit(solution)/shard_map/mbn,bq->mnq/dot_general | solution.py:53
  144.0 7.2 multiply_add_fusion
  151.2 6.6 pad_maximum_fusion
  157.8 23.1 %fusion.9 = bf16[2,32,128,256]{2,1,3,0:T(8,128)(2,1)} fusion(f32[2,256,64,128]{3,1,2,0:T(8,128)S(1)} %pad_maximum_fusion, f32[1,64,2,32]{1,3,0,2:T(8,128)S(1)} %get-tuple-element.16, f32[1,64,2,32]{1,3,0,2:T(8,128)S(1)} %get-tuple-element.15), kind=kOutput, calls=%fused_computation.27 | convolution fusion | flops 1612718080 | bytes 21004288 | tf_op jit(solution)/shard_map/rmnk,rnqj->qjkm/dot_general | solution.py:64
  180.9 7.3 %convert_element_type.72 = bf16[2,4096,32,8]{1,3,2,0:T(8,128)(2,1)} reshape(bf16[2,32,128,256]{2,1,3,0:T(8,128)(2,1)} %fusion.9) | data formatting | bytes 8388608 | tf_op jit(solution)/shard_map/convert_element_type | solution.py:66
  188.2 22.8 %copy.35 = bf16[2,4096,32,8]{2,3,0,1:T(8,128)(2,1)} copy(bf16[2,4096,32,8]{1,3,2,0:T(8,128)(2,1)} %convert_element_type.72) | data formatting | bytes 8388608 | tf_op jit(solution)/shard_map/convert_element_type | solution.py:66
  211.0 20.8 %reshape.331 = bf16[16,2,65536]{2,1,0:T(2,128)(2,1)} reshape(bf16[4096,2,8,32]{3,2,1,0:T(8,128)(2,1)} %bitcast.111) | data formatting | bytes 8388608
  231.8 5.3 all-to-all-start.1
  238.5 90.9 %all-to-all-done.1 = bf16[16,2,65536]{2,1,0:T(2,128)(2,1)} async-done(((bf16[16,2,65536]{2,1,0:T(2,128)(2,1)}), bf16[16,2,65536]{2,1,0:T(2,128)(2,1)}, u32[]{:S(2)}, u32[]{:S(2)}) %all-to-all-start.1) | async-done | bytes 4194336 | tf_op jit(solution)/shard_map/all_to_all | solution.py:103
  329.3 15.9 %reshape.332 = bf16[4096,2,8,32]{3,2,1,0:T(8,128)(2,1)} reshape(bf16[16,2,65536]{2,1,0:T(2,128)(2,1)} %all-to-all-done.1) | data formatting | bytes 8388608
  345.2 16.1 %copy.36 = bf16[2,16,256,32,8]{2,3,4,1,0:T(8,128)(2,1)} copy(bf16[2,16,256,32,8]{3,4,0,2,1:T(8,128)(2,1)} %bitcast.112) | data formatting | bytes 8388608 | tf_op jit(solution)/shard_map/all_to_all | solution.py:103
  361.4 5.0 gather_fusion.1
  366.4 9.0 %copy_select_fusion = bf16[2,256,32,4,32]{1,4,3,2,0:T(8,128)(2,1)} fusion(bf16[2,256,32,4,32]{1,2,0,4,3:T(8,128)(2,1)} %bitcast.117, pred[4,32]{1,0:T(4,128)(4,1)S(1)} %compare_and_fusion.2), kind=kLoop, calls=%fused_computation.28 | loop fusion | flops 2097152 | bytes 8388736 | tf_op jit(solution)/shard_map/jit(_take)/select_n | solution.py:106
  375.4 6.8 gather_fusion.3
  382.1 7.0 gather_fusion.2
  389.2 55.0 %copy.38 = bf16[8,2,256,32,32]{3,4,0,2,1:T(8,128)(2,1)} copy(bf16[8,2,256,32,32]{2,4,3,1,0:T(8,128)(2,1)} %gather_fusion.2) | data formatting | bytes 16777216 | tf_op jit(solution)/shard_map/jit(_take)/gather | solution.py:109
  444.2 44.3 %copy.39 = bf16[8,2,256,32,32]{4,3,0,2,1:T(8,128)(2,1)} copy(bf16[8,2,256,32,32]{2,4,3,1,0:T(8,128)(2,1)} %gather_fusion.3) | data formatting | bytes 16777216 | tf_op jit(solution)/shard_map/jit(_take)/gather | solution.py:110
  488.5 23.3 %select_bitcast_fusion.1 = bf16[2,256,32,8,32]{2,4,3,1,0:T(8,128)(2,1)} fusion(bf16[8,2,256,32,32]{3,4,0,2,1:T(8,128)(2,1)} %copy.38, pred[8]{0:T(512)(128)(4,1)S(1)} %get-tuple-element.17), kind=kLoop, calls=%fused_computation.5 | loop fusion | flops 4194304 | bytes 16777224 | tf_op jit(solution)/shard_map/jit(_take)/select_n | solution.py:109
  511.8 23.3 %select_bitcast_fusion = bf16[2,256,32,8,32]{4,2,3,1,0:T(8,128)(2,1)} fusion(bf16[8,2,256,32,32]{4,3,0,2,1:T(8,128)(2,1)} %copy.39, pred[8]{0:T(512)(128)(4,1)S(1)} %get-tuple-element.6), kind=kLoop, calls=%fused_computation.4 | loop fusion | flops 4194304 | bytes 16777224 | tf_op jit(solution)/shard_map/jit(_take)/select_n | solution.py:110
  535.1 24.6 %fusion.3 = f32[256,8,32,32]{3,2,1,0:T(8,128)} fusion(bf16[2,256,32,8,32]{2,4,3,1,0:T(8,128)(2,1)} %select_bitcast_fusion.1, bf16[2,256,32,8,32]{4,2,3,1,0:T(8,128)(2,1)} %select_bitcast_fusion), kind=kOutput, calls=%fused_computation.15 | convolution fusion | flops 134217728 | bytes 41943040 | tf_op jit(solution)/shard_map/cspa,cspb->cpab/dot_general | solution.py:113
  559.7 24.3 %fusion.4 = f32[256,8,32,32]{3,2,1,0:T(8,128)} fusion(bf16[2,256,32,8,32]{2,4,3,1,0:T(8,128)(2,1)} %select_bitcast_fusion.1, bf16[2,256,32,8,32]{4,2,3,1,0:T(8,128)(2,1)} %select_bitcast_fusion), kind=kOutput, calls=%fused_computation.16 | convolution fusion | flops 134217728 | bytes 41943040 | tf_op jit(solution)/shard_map/cspa,cspb->cpab/dot_general | solution.py:113
  584.0 33.9 %fusion.8 = f32[256,8,32,32]{3,2,1,0:T(8,128)} fusion(f32[256,8,32,32]{3,2,1,0:T(8,128)} %fusion.3, bf16[2,256,32,8,32]{4,2,3,1,0:T(8,128)(2,1)} %select_bitcast_fusion, bf16[2,256,32,8,32]{2,4,3,1,0:T(8,128)(2,1)} %select_bitcast_fusion.1), kind=kOutput, calls=%fused_computation.20 | convolution fusion | flops 136314880 | bytes 75497472 | tf_op jit(solution)/shard_map/cspa,cspb->cpab/dot_general | solution.py:113
  617.9 25.1 %copy.41 = f32[256,8,32,32]{0,3,2,1:T(8,128)} copy(f32[256,8,32,32]{3,2,1,0:T(8,128)} %fusion.8) | data formatting | bytes 16777216 | tf_op jit(solution)/shard_map/sub | solution.py:118
  643.0 33.9 %fusion.7 = f32[256,8,32,32]{3,2,1,0:T(8,128)} fusion(f32[256,8,32,32]{3,2,1,0:T(8,128)} %fusion.4, bf16[2,256,32,8,32]{4,2,3,1,0:T(8,128)(2,1)} %select_bitcast_fusion, bf16[2,256,32,8,32]{2,4,3,1,0:T(8,128)(2,1)} %select_bitcast_fusion.1), kind=kOutput, calls=%fused_computation.19 | convolution fusion | flops 136314880 | bytes 75497472 | tf_op jit(solution)/shard_map/cspa,cspb->cpab/dot_general | solution.py:113
  676.8 25.1 %copy.40 = f32[256,8,32,32]{0,3,2,1:T(8,128)} copy(f32[256,8,32,32]{3,2,1,0:T(8,128)} %fusion.7) | data formatting | bytes 16777216 | tf_op jit(solution)/shard_map/add | solution.py:117
  701.9 11.4 %maximum_multiply_fusion = f32[2,256,8,1024]{1,3,2,0:T(8,128)} fusion(f32[1,256,8,1024]{1,3,2,0:T(8,128)} %bitcast.114, f32[1,256,8,1024]{1,3,2,0:T(8,128)} %bitcast.115), kind=kLoop, calls=%fused_computation.11 | loop fusion | flops 8388608 | bytes 33554432 | tf_op jit(solution)/shard_map/mul | solution.py:119
  713.3 16.9 %copy.42 = f32[2,256,8,1024]{3,2,1,0:T(8,128)} copy(f32[2,256,8,1024]{1,3,2,0:T(8,128)} %maximum_multiply_fusion) | data formatting | bytes 33554432 | tf_op jit(solution)/shard_map/mul | solution.py:119
  (22 shorter events, 3.2 us)
Async XLA Ops:
  0.0 237.1 %copy-start = (s32[64]{0:T(128)S(1)}, s32[64]{0:T(128)}, u32[]{:S(2)}) copy-start(s32[64]{0:T(128)} %param.8) | copy-start | bytes 772
  0.0 99.2 %all-to-all-start = ((bf16[16,8,16384]{2,1,0:T(8,128)(2,1)}), bf16[16,8,16384]{2,1,0:T(8,128)(2,1)}, u32[]{:S(2)}, u32[]{:S(2)}) async-start(bf16[16,8,16384]{2,1,0:T(8,128)(2,1)} %bitcast.118), calls=%async_computation | async-start | bytes 8388608 | tf_op jit(solution)/shard_map/all_to_all | solution.py:89
  211.0 27.4 %copy-start.2 = (s32[8,2]{0,1:T(2,128)S(1)}, s32[8,2]{0,1:T(2,128)}, u32[]{:S(2)}) copy-start(s32[8,2]{0,1:T(2,128)} %param.9) | copy-start | bytes 196
  231.8 97.6 %all-to-all-start.1 = ((bf16[16,2,65536]{2,1,0:T(2,128)(2,1)}), bf16[16,2,65536]{2,1,0:T(2,128)(2,1)}, u32[]{:S(2)}, u32[]{:S(2)}) async-start(bf16[16,2,65536]{2,1,0:T(2,128)(2,1)} %reshape.331), calls=%async_computation.1 | async-start | bytes 8388608 | tf_op jit(solution)/shard_map/all_to_all | solution.py:103
  701.9 28.3 %copy-start.1 = (s32[64]{0:T(128)S(1)}, s32[64]{0:T(128)}, u32[]{:S(2)}) copy-start(s32[64]{0:T(128)} %param.8) | copy-start | bytes 772
where the time goes:
time: 740 us; the launch traced here: 731 us
  local copies, waits for them, and re-layouts  298 us (40%)
  waiting for transfers between devices  182 us (25%)
  matrix products  149 us (20%)
  other arithmetic  89.3 us (12%)
  starting transfers between devices  12 us (2%)
    dot_general x4, matrix products, product(): jnp.einsum('cspa,cspb->cpab', operand_one, operand_two, preferred_element...  117 us
    all_to_all x1, waiting for transfers between devices, shards(): lax.all_to_all(spectra_local, 'row', split_axis=1, concat_axis=3, tiled=T...  90.9 us
    all_to_all x1, waiting for transfers between devices, shards(): lax.all_to_all(voltages, 'row', split_axis=0, concat_axis=1, tiled=True)  90.6 us
    gather x2, local copies, waits for them, and re-layouts, shards(): left_blocks = jnp.take(tiled, pair_list[:, 0], axis=3)  62.1 us
    gather x2, local copies, waits for them, and re-layouts, shards(): right_blocks = jnp.take(tiled, pair_list[:, 1], axis=3)  51.1 us
    unnamed x8, local copies, waits for them, and re-layouts  36.7 us
    convert_element_type x2, local copies, waits for them, and re-layouts, transform(): return result.reshape(2, channel_count, row_count).astype(jnp.bfloat16)  30.1 us
    another operation x2, local copies, waits for them, and re-layouts, transform(): folded = filtered.reshape(row_count, inner_len, outer_len)  27.8 us
  transfers between devices with their start and end apart: 2, of which 2 were waited for; matrix products, arithmetic and copies ran while one was open for 0% of the time, Pallas kernels for 0%

commit v1 on v0

v1 whole, which is shorter than its diff:
```python
import functools
import math

import jax
import jax.numpy as jnp
import numpy as np
from jax import lax
from jax.experimental import pallas as pl
from jax.experimental.pallas import tpu as pltpu
from jax.sharding import PartitionSpec as P

BLOCK_SIZE = 32
LANES = 128
RADIX = 64
HALF = RADIX // 2
ROWS = 16
VMEM_BYTES = 56 * 1024 * 1024


def dft_tables(length):
    a = np.arange(LANES)
    k1 = np.arange(HALF + 1)
    angle = 2.0 * np.pi * ((k1[:, None] * a[None, :]) % length) / length
    twist = np.stack([np.cos(angle), np.sin(angle)]).astype(np.float32)
    low = np.arange(RADIX)
    high = LANES - 1 - low

    def rows(k2, sign):
        ang = 2.0 * np.pi * ((k2[:, None] * a[None, :]) % LANES) / LANES
        c, s = np.cos(ang), np.sin(ang)
        real = np.concatenate([c, s], 1)
        imag = np.concatenate([-s, c], 1) * sign
        return [real, imag]

    table = np.concatenate(rows(low, 1.0) + rows(high, -1.0), 0) / math.sqrt(length)
    table_hi = table.astype(np.float32).astype(jnp.bfloat16)
    table_lo = (table - table_hi.astype(np.float64)).astype(np.float32).astype(jnp.bfloat16)
    return twist, np.stack([table_hi, table_lo])


def add(x, y):
    return (x[0] + y[0], none_add(x[1], y[1]))


def none_add(x, y):
    if x is None:
        return y
    return x if y is None else x + y


def none_sub(x, y):
    if y is None:
        return x
    return -y if x is None else x - y


def sub(x, y):
    return (x[0] - y[0], none_sub(x[1], y[1]))


def times(x, c, s):
    re, im = x
    if abs(s) < 1e-12:
        return x if c > 0 else (-re, None if im is None else -im)
    if abs(c) < 1e-12:
        if s > 0:
            return (jnp.zeros_like(re) if im is None else im, -re)
        return (jnp.zeros_like(re) if im is None else -im, re)
    if im is None:
        return (re * c, re * (-s))
    if abs(abs(c) - abs(s)) < 1e-12:
        r = abs(c)
        sc, ss = (1 if c > 0 else -1), (1 if s > 0 else -1)
        p = re + im if sc == ss else re - im
        q = im - re if sc == ss else im + re
        return (p * (r * sc), q * (r * sc))
    return (re * c + im * s, im * c - re * s)


def fft_list(xs):
    n = len(xs)
    if n == 1:
        return xs
    even, odd = fft_list(xs[0::2]), fft_list(xs[1::2])
    out = [None] * n
    for k in range(n // 2):
        ang = 2.0 * math.pi * k / n
        t = times(odd[k], math.cos(ang), math.sin(ang))
        out[k] = add(even[k], t)
        out[k + n // 2] = sub(even[k], t)
    return out


def real_dft64(xs):
    first = [fft_list([(xs[8 * b1 + b0], None) for b1 in range(8)]) for b0 in range(8)]
    out = {}
    for k in range(5):
        terms = []
        for b0 in range(8):
            ang = 2.0 * math.pi * b0 * k / 64
            terms.append(times(first[b0][k], math.cos(ang), math.sin(ang)))
        res = fft_list(terms)
        for j in range(8):
            k1 = k + 8 * j
            if k1 <= 32:
                out[k1] = res[j]
            elif 64 - k1 not in out:
                re, im = res[j]
                out[64 - k1] = (re, None if im is None else -im)
    return out


def fft_kernel(now_ref, past_ref, taps_ref, twist_ref, table_ref, out_ref, z_hi, z_lo, spec):
    inputs = now_ref.shape[0]
    spectra = now_ref.shape[1] // (RADIX * LANES)
    length = RADIX * LANES
    group = out_ref.shape[3]
    groups = out_ref.shape[0]

    for s in range(spectra):

        @pl.loop(0, inputs // ROWS)
        def _(step):
            r0 = pl.multiple_of(step * ROWS, ROWS)
            xs = []
            for b in range(RADIX):
                lanes = b * LANES
                total = None
                for t in range(3):
                    block = s + t - 2
                    if block < 0:
                        ref, off = past_ref, (block + 2) * length + lanes
                    else:
                        ref, off = now_ref, block * length + lanes
                    term = taps_ref[t : t + 1, lanes : lanes + LANES] * ref[
                        pl.ds(r0, ROWS), off : off + LANES
                    ].astype(jnp.float32)
                    total = term if total is None else total + term
                xs.append(total)
            values = real_dft64(xs)
            for k1 in range(HALF + 1):
                re, im = values[k1]
                if k1 == 0:
                    parts = (re, jnp.zeros_like(re))
                else:
                    c = twist_ref[0, k1 : k1 + 1, :]
                    n = twist_ref[1, k1 : k1 + 1, :]
                    if im is None:
                        parts = (re * c, -(re * n))
                    else:
                        parts = (re * c + im * n, im * c - re * n)
                for i, part in enumerate(parts):
                    hi = part.astype(jnp.bfloat16)
                    lo = (part - hi.astype(jnp.float32)).astype(jnp.bfloat16)
                    z_hi[k1, pl.ds(r0, ROWS), i * LANES : (i + 1) * LANES] = hi
                    z_lo[k1, pl.ds(r0, ROWS), i * LANES : (i + 1) * LANES] = lo

        def second(k1, rows):
            dims = (((1,), (1,)), ((), ()))
            hi, lo = z_hi[k1], z_lo[k1]
            w_hi, w_lo = table_ref[0, :rows, :], table_ref[1, :rows, :]
            dot = functools.partial(
                lax.dot_general, dimension_numbers=dims, preferred_element_type=jnp.float32
            )
            o = dot(w_hi, hi) + dot(w_hi, lo) + dot(w_lo, hi)
            for c in range(2):
                spec[c, pl.ds(k1, RADIX, stride=RADIX), :] = o[c * RADIX : (c + 1) * RADIX]
                if rows > 2 * RADIX:
                    spec[c, pl.ds(RADIX - k1, RADIX, stride=RADIX), :] = o[
                        (2 + c) * RADIX : (3 + c) * RADIX
                    ]

        second(0, 2 * RADIX)
        second(HALF, 2 * RADIX)

        @pl.loop(1, HALF)
        def _(k1):
            second(k1, 4 * RADIX)

        @pl.loop(0, groups)
        def _(g):
            for c in range(2):
                out_ref[g, s, c] = spec[c, pl.ds(pl.multiple_of(g * group, group), group), :].astype(
                    jnp.bfloat16
                )


def spectra_of(now, past, taps, groups):
    inputs, samples = now.shape
    length = taps.shape[1]
    assert length == RADIX * LANES and inputs == LANES and taps.shape[0] == 3
    spectra = samples // length
    assert spectra == 2
    channels = length // 2
    twist, table = dft_tables(length)
    vmem = pl.BlockSpec(memory_space=pltpu.VMEM)
    return pl.pallas_call(
        fft_kernel,
        out_shape=jax.ShapeDtypeStruct(
            (groups, spectra, 2, channels // groups, inputs), jnp.bfloat16
        ),
        in_specs=[vmem] * 5,
        out_specs=vmem,
        scratch_shapes=[
            pltpu.VMEM((HALF + 1, inputs, 2 * LANES), jnp.bfloat16),
            pltpu.VMEM((HALF + 1, inputs, 2 * LANES), jnp.bfloat16),
            pltpu.VMEM((2, channels, inputs), jnp.float32),
        ],
        compiler_params=pltpu.CompilerParams(vmem_limit_bytes=VMEM_BYTES),
        cost_estimate=pl.CostEstimate(
            flops=10_000_000_000, bytes_accessed=12_000_000, transcendentals=0
        ),
    )(now, past, taps, jnp.asarray(twist), jnp.asarray(table))


def pair_kernel(scale, pair_ref, data_ref, pick_ref, out_ref, turned, gram, rows_ref):
    depth, chunk, inputs = data_ref.shape
    pairs = out_ref.shape[2]
    half = depth // 2
    data = data_ref[...].reshape(depth * chunk, inputs)
    turned[...] = jnp.dot(data, pick_ref[...], preferred_element_type=jnp.float32)
    lane_group = lax.broadcasted_iota(jnp.int32, (8, LANES), 1) // BLOCK_SIZE

    @pl.loop(0, chunk)
    def _(ch):
        re = turned[pl.ds(ch, half, stride=2 * chunk), :]
        im = turned[pl.ds(chunk + ch, half, stride=2 * chunk), :]
        left = jnp.concatenate([re, im], 0).astype(jnp.bfloat16)
        swapped = jnp.concatenate([-im, re], 0).astype(jnp.bfloat16)
        dims = (((0,), (0,)), ((), ()))
        for c, right in enumerate((left, swapped)):
            gram[c] = lax.dot_general(left, right, dims, preferred_element_type=jnp.float32)
        for c in range(2):
            for p in range(pairs):
                first, second = pair_ref[p, 0], pair_ref[p, 1]
                tile = None
                for j in range(4):
                    piece = gram[c, pl.ds(first * BLOCK_SIZE + j, 8, stride=4), :]
                    amount = lax.rem(j - second + 4, 4) * BLOCK_SIZE
                    piece = pltpu.roll(piece, amount, 1)
                    tile = piece if tile is None else jnp.where(lane_group == j, piece, tile)
                rows_ref[c, pl.ds(p, 8, stride=pairs), :] = tile
            for t in range(8):
                out_ref[c, ch, :, t * LANES : (t + 1) * LANES] = (
                    rows_ref[c, t * pairs : (t + 1) * pairs, :] * scale
                )


def visibilities_of(gathered, pick, pair_list, scale):
    depth, channels, inputs = gathered.shape
    pairs = pair_list.shape[0]
    chunk = min(32, channels)
    return pl.pallas_call(
        functools.partial(pair_kernel, scale),
        grid_spec=pltpu.PrefetchScalarGridSpec(
            num_scalar_prefetch=1,
            grid=(channels // chunk,),
            in_specs=[
                pl.BlockSpec((depth, chunk, inputs), lambda i, _: (0, i, 0)),
                pl.BlockSpec((inputs, inputs), lambda i, _: (0, 0)),
            ],
            out_specs=pl.BlockSpec(
                (2, chunk, pairs, BLOCK_SIZE * BLOCK_SIZE), lambda i, _: (0, i, 0, 0)
            ),
            scratch_shapes=[
                pltpu.VMEM((depth * chunk, inputs), jnp.float32),
                pltpu.VMEM((2, inputs, inputs), jnp.float32),
                pltpu.VMEM((2, 8 * pairs, LANES), jnp.float32),
            ],
        ),
        out_shape=jax.ShapeDtypeStruct(
            (2, channels, pairs, BLOCK_SIZE * BLOCK_SIZE), jnp.float32
        ),
        compiler_params=pltpu.CompilerParams(
            vmem_limit_bytes=VMEM_BYTES, dimension_semantics=("arbitrary",)
        ),
        cost_estimate=pl.CostEstimate(
            flops=4_000_000_000, bytes_accessed=20_000_000, transcendentals=0
        ),
    )(pair_list, gathered, pick)


def input_order(station_order):
    return (2 * station_order[:, None] + jnp.arange(2, dtype=jnp.int32)[None, :]).reshape(-1)


def shards(row_count, voltages, taps, station_order, pair_list):
    order = input_order(station_order)
    inputs = voltages.shape[0]
    pick = (jnp.arange(inputs, dtype=jnp.int32)[:, None] == order[None, :]).astype(jnp.bfloat16)
    past = lax.ppermute(voltages, "row", [(i, i + 1) for i in range(row_count - 1)])
    spectra = spectra_of(voltages, past, taps, row_count)
    gathered = lax.all_to_all(spectra, "row", split_axis=0, concat_axis=0, tiled=True)
    spectra_total = row_count * spectra.shape[1]
    gathered = gathered.reshape(spectra_total * 2, spectra.shape[3], inputs)
    return visibilities_of(gathered, pick, pair_list, 1.0 / spectra_total)


def solution(mesh):
    placed = (P("grp", "row"), P(), P("grp"), P("grp", None))
    return jax.shard_map(
        functools.partial(shards, mesh.shape["row"]),
        mesh=mesh,
        in_specs=placed,
        out_specs=P(None, "row", "grp", None),
        check_vma=False,
    )
```

time: 740 us -> 290 us (0.39); the launches traced: 731 us -> 290 us
  local copies, waits for them, and re-layouts: 298 us -> 2.83 us
  matrix products: 149 us -> 0 us
  Pallas kernels: 0 us -> 138 us
  other arithmetic: 89.3 us -> 0.7 us
  waiting for transfers between devices: 182 us -> 137 us
    dot_general x6 -> x0, matrix products: 149 us -> none  [the longest x4 117 us: product(): jnp.einsum('cspa,cspb->cpab', operand_one, operand_two, preferred_element...]
    pallas_call x0 -> x2, Pallas kernels: none -> 138 us  [the longest x1 103 us: visibilities_of(): pl.pallas_call(functools.partial(pair_kernel, scale), grid_spec=pltpu.Pre...]
    gather x7 -> x0, local copies, waits for them, and re-layouts: 119 us -> none  [the longest x2 62.1 us: shards(): left_blocks = jnp.take(tiled, pair_list[:, 0], axis=3)]
    all_to_all x2 -> x1, waiting for transfers between devices: 182 us -> 90.9 us  [shards(): lax.all_to_all(spectra, 'row', split_axis=0, concat_axis=0, tiled=True)]
    select_n x5 -> x0, other arithmetic: 55.6 us -> none  [the longest x1 23.3 us: shards(): left_blocks = jnp.take(tiled, pair_list[:, 0], axis=3)]
    ppermute x0 -> x1, waiting for transfers between devices: none -> 45.7 us  [shards(): lax.ppermute(voltages, 'row', [(i, i + 1) for i in range(row_count - 1)])]
    unnamed x8 -> x7, local copies, waits for them, and re-layouts: 36.7 us -> 2.69 us
    convert_element_type x2 -> x0, local copies, waits for them, and re-layouts: 30.1 us -> none  [transform(): return result.reshape(2, channel_count, row_count).astype(jnp.bfloat16)]
  transfers between devices with their start and end apart: 2 -> 2, of which waited for: 2 -> 2; matrix products, arithmetic and copies ran while one was open for 0% -> 1% of each run, Pallas kernels for 0% -> 0%
where the time goes in v1:
time: 290 us
  Pallas kernels  138 us (48%)
  waiting for transfers between devices  137 us (47%)
  starting transfers between devices  11 us (4%)
    pallas_call x1, Pallas kernels, visibilities_of(): pl.pallas_call(functools.partial(pair_kernel, scale), grid_spec=pltpu.Pre...  103 us
    all_to_all x1, waiting for transfers between devices, shards(): lax.all_to_all(spectra, 'row', split_axis=0, concat_axis=0, tiled=True)  90.9 us
    ppermute x1, waiting for transfers between devices, shards(): lax.ppermute(voltages, 'row', [(i, i + 1) for i in range(row_count - 1)])  45.7 us
    pallas_call x1, Pallas kernels, spectra_of(): pl.pallas_call(fft_kernel, out_shape=jax.ShapeDtypeStruct((groups, spectr...  35.7 us
    all_to_all x1, starting transfers between devices, shards(): lax.all_to_all(spectra, 'row', split_axis=0, concat_axis=0, tiled=True)  7.23 us
  transfers between devices with their start and end apart: 2, of which 2 were waited for; matrix products, arithmetic and copies ran while one was open for 1% of the time, Pallas kernels for 0%

profile of v1, /device:TPU:11, one launch (start us, length us, event | category | flops | bytes accessed | tf_op | source)
XLA Modules:
  0.0 289.5 jit_solution(247451184987032334)
XLA Ops:
  0.0 3.7 %collective-permute-start = (bf16[128,16384]{1,0:T(8,128)(2,1)}, bf16[128,16384]{1,0:T(8,128)(2,1)S(1)}, u32[]{:S(2)}, u32[]{:S(2)}) collective-permute-start(bf16[128,16384]{1,0:T(8,128)(2,1)} %now_ref.1), channel_id=1, source_target_pairs={{0,1},{1,2},{2,3},{3,4},{4,5},{5,6},{6,7},{7,8},{8,9},{9,10},{10,1... | collective-permute-start | bytes 12582920 | tf_op jit(solution)/shard_map/ppermute | solution.py:291
  3.7 45.7 %collective-permute-done.past_ref = bf16[128,16384]{1,0:T(8,128)(2,1)S(1)} collective-permute-done((bf16[128,16384]{1,0:T(8,128)(2,1)}, bf16[128,16384]{1,0:T(8,128)(2,1)S(1)}, u32[]{:S(2)}, u32[]{:S(2)}) %collective-permute-start) | collective-permute-done | bytes 4194336 | tf_op jit(solution)/shard_map/ppermute | solution.py:291
  49.5 0.0 copy-start.1
  49.5 2.0 copy-done.1
  51.5 35.7 %shard_map.64 = bf16[16,2,2,256,128]{4,3,2,1,0:T(8,128)(2,1)} custom-call(bf16[128,16384]{1,0:T(8,128)(2,1)} %now_ref.1, bf16[128,16384]{1,0:T(8,128)(2,1)} %copy-done.1, f32[3,8192]{1,0:T(4,128)} %taps_ref.1, f32[2,33,128]{2,1,0:T(8,128)} %constant.6.clone.twist_ref, bf16[2,256,256]{2,1,0:T(8,128)(2,1)} %constant.7.clone.table_ref), custom_call_target="tpu_custom_call" | custom-call | flops 10000000000 | bytes 12000000 | tf_op jit(solution)/shard_map/pallas_call | solution.py:197
  87.2 0.0 copy-start
  87.2 0.0 copy-start.2
  87.2 7.2 %all-to-all-start = ((bf16[16,2,2,256,128]{4,3,2,1,0:T(8,128)(2,1)}), bf16[16,2,2,256,128]{4,3,2,1,0:T(8,128)(2,1)}, u32[]{:S(2)}, u32[]{:S(2)}) async-start(bf16[16,2,2,256,128]{4,3,2,1,0:T(8,128)(2,1)} %shard_map.64), calls=%async_computation | async-start | bytes 8388608 | tf_op jit(solution)/shard_map/all_to_all | solution.py:293
  94.4 0.0 copy-done
  94.4 0.7 copy.8.pair_ref
  95.1 0.0 copy-done.2
  95.1 0.1 iota_add_fusion
  95.2 0.1 add.23
  95.3 0.6 fusion.pick_ref
  95.9 90.9 %all-to-all-done = bf16[16,2,2,256,128]{4,3,2,1,0:T(8,128)(2,1)} async-done(((bf16[16,2,2,256,128]{4,3,2,1,0:T(8,128)(2,1)}), bf16[16,2,2,256,128]{4,3,2,1,0:T(8,128)(2,1)}, u32[]{:S(2)}, u32[]{:S(2)}) %all-to-all-start) | async-done | bytes 4194336 | tf_op jit(solution)/shard_map/all_to_all | solution.py:293
  186.9 102.6 %shard_map.65 = f32[2,256,8,1024]{3,2,1,0:T(8,128)} custom-call(s32[8,2]{1,0:T(8,128)} %copy.8.pair_ref, bf16[64,256,128]{2,1,0:T(8,128)(2,1)} %bitcast.data_ref, bf16[128,128]{1,0:T(8,128)(2,1)} %fusion.pick_ref), custom_call_target="tpu_custom_call" | custom-call | flops 4000000000 | bytes 20000000 | tf_op jit(solution)/shard_map/pallas_call | solution.py:253
  (1 shorter events, 0.0 us)
Async XLA Ops:
  0.0 49.5 %collective-permute-start = (bf16[128,16384]{1,0:T(8,128)(2,1)}, bf16[128,16384]{1,0:T(8,128)(2,1)S(1)}, u32[]{:S(2)}, u32[]{:S(2)}) collective-permute-start(bf16[128,16384]{1,0:T(8,128)(2,1)} %now_ref.1), channel_id=1, source_target_pairs={{0,1},{1,2},{2,3},{3,4},{4,5},{5,6},{6,7},{7,8},{8,9},{9,10},{10,1... | collective-permute-start | bytes 12582920 | tf_op jit(solution)/shard_map/ppermute | solution.py:291
  49.5 2.0 copy-start.1
  87.2 7.2 %copy-start = (s32[8,2]{0,1:T(2,128)S(1)}, s32[8,2]{0,1:T(2,128)}, u32[]{:S(2)}) copy-start(s32[8,2]{0,1:T(2,128)} %param.9) | copy-start | bytes 196
  87.2 7.9 %copy-start.2 = (s32[64]{0:T(128)S(1)}, s32[64]{0:T(128)}, u32[]{:S(2)}) copy-start(s32[64]{0:T(128)} %param.8) | copy-start | bytes 772
  87.2 99.7 %all-to-all-start = ((bf16[16,2,2,256,128]{4,3,2,1,0:T(8,128)(2,1)}), bf16[16,2,2,256,128]{4,3,2,1,0:T(8,128)(2,1)}, u32[]{:S(2)}, u32[]{:S(2)}) async-start(bf16[16,2,2,256,128]{4,3,2,1,0:T(8,128)(2,1)} %shard_map.64), calls=%async_computation | async-start | bytes 8388608 | tf_op jit(solution)/shard_map/all_to_all | solution.py:293

commit v2 on v1

v2 whole, which is shorter than its diff:
```python
import functools
import math

import jax
import jax.numpy as jnp
import numpy as np
from jax import lax
from jax.experimental import pallas as pl
from jax.experimental.pallas import tpu as pltpu
from jax.sharding import PartitionSpec as P

BLOCK_SIZE = 32
LANES = 128
RADIX = 64
HALF = RADIX // 2
ROWS = 16
UNROLL = 16
PIECES = 2
VMEM_BYTES = 56 * 1024 * 1024


def dft_tables(length):
    a = np.arange(LANES)
    k1 = np.arange(HALF + 1)
    angle = 2.0 * np.pi * ((k1[:, None] * a[None, :]) % length) / length
    twist = np.stack([np.cos(angle), np.sin(angle)]).astype(np.float32)
    low = np.arange(RADIX)
    high = LANES - 1 - low

    def rows(k2, sign):
        ang = 2.0 * np.pi * ((k2[:, None] * a[None, :]) % LANES) / LANES
        c, s = np.cos(ang), np.sin(ang)
        real = np.concatenate([c, s], 1)
        imag = np.concatenate([-s, c], 1) * sign
        return [real, imag]

    table = np.concatenate(rows(low, 1.0) + rows(high, -1.0), 0) / math.sqrt(length)
    table_hi = table.astype(np.float32).astype(jnp.bfloat16)
    table_lo = (table - table_hi.astype(np.float64)).astype(np.float32).astype(jnp.bfloat16)
    return twist, np.stack([table_hi, table_lo])


def add(x, y):
    return (x[0] + y[0], none_add(x[1], y[1]))


def none_add(x, y):
    if x is None:
        return y
    return x if y is None else x + y


def none_sub(x, y):
    if y is None:
        return x
    return -y if x is None else x - y


def sub(x, y):
    return (x[0] - y[0], none_sub(x[1], y[1]))


def times(x, c, s):
    re, im = x
    if abs(s) < 1e-12:
        return x if c > 0 else (-re, None if im is None else -im)
    if abs(c) < 1e-12:
        if s > 0:
            return (jnp.zeros_like(re) if im is None else im, -re)
        return (jnp.zeros_like(re) if im is None else -im, re)
    if im is None:
        return (re * c, re * (-s))
    if abs(abs(c) - abs(s)) < 1e-12:
        r = abs(c)
        sc, ss = (1 if c > 0 else -1), (1 if s > 0 else -1)
        p = re + im if sc == ss else re - im
        q = im - re if sc == ss else im + re
        return (p * (r * sc), q * (r * sc))
    return (re * c + im * s, im * c - re * s)


def fft_list(xs):
    n = len(xs)
    if n == 1:
        return xs
    even, odd = fft_list(xs[0::2]), fft_list(xs[1::2])
    out = [None] * n
    for k in range(n // 2):
        ang = 2.0 * math.pi * k / n
        t = times(odd[k], math.cos(ang), math.sin(ang))
        out[k] = add(even[k], t)
        out[k + n // 2] = sub(even[k], t)
    return out


def real_dft64(xs):
    first = [fft_list([(xs[8 * b1 + b0], None) for b1 in range(8)]) for b0 in range(8)]
    out = {}
    for k in range(5):
        terms = []
        for b0 in range(8):
            ang = 2.0 * math.pi * b0 * k / 64
            terms.append(times(first[b0][k], math.cos(ang), math.sin(ang)))
        res = fft_list(terms)
        for j in range(8):
            k1 = k + 8 * j
            if k1 <= 32:
                out[k1] = res[j]
            elif 64 - k1 not in out:
                re, im = res[j]
                out[64 - k1] = (re, None if im is None else -im)
    return out


def fft_kernel(old_ref, mid_ref, new_ref, taps_ref, twist_ref, table_ref, *rest):
    *out_refs, z_hi, z_lo, spec = rest
    inputs = new_ref.shape[0]
    groups = out_refs[0].shape[0]
    group = sum(ref.shape[2] for ref in out_refs)

    @pl.loop(0, inputs // ROWS)
    def _(step):
        r0 = pl.multiple_of(step * ROWS, ROWS)
        xs = []
        for b in range(RADIX):
            lanes = slice(b * LANES, (b + 1) * LANES)
            total = None
            for t, ref in enumerate((old_ref, mid_ref, new_ref)):
                term = taps_ref[t : t + 1, lanes] * ref[pl.ds(r0, ROWS), lanes].astype(jnp.float32)
                total = term if total is None else total + term
            xs.append(total)
        values = real_dft64(xs)
        for k1 in range(HALF + 1):
            re, im = values[k1]
            if k1 == 0:
                parts = (re, jnp.zeros_like(re))
            else:
                c = twist_ref[0, k1 : k1 + 1, :]
                n = twist_ref[1, k1 : k1 + 1, :]
                if im is None:
                    parts = (re * c, -(re * n))
                else:
                    parts = (re * c + im * n, im * c - re * n)
            for i, part in enumerate(parts):
                hi = part.astype(jnp.bfloat16)
                lo = (part - hi.astype(jnp.float32)).astype(jnp.bfloat16)
                z_hi[k1, pl.ds(r0, ROWS), i * LANES : (i + 1) * LANES] = hi
                z_lo[k1, pl.ds(r0, ROWS), i * LANES : (i + 1) * LANES] = lo

    def second(k1, rows):
        dims = (((1,), (1,)), ((), ()))
        hi, lo = z_hi[k1], z_lo[k1]
        w_hi, w_lo = table_ref[0, :rows, :], table_ref[1, :rows, :]
        dot = functools.partial(
            lax.dot_general, dimension_numbers=dims, preferred_element_type=jnp.float32
        )
        o = dot(w_hi, hi) + dot(w_hi, lo) + dot(w_lo, hi)
        for c in range(2):
            spec[c, pl.ds(k1, RADIX, stride=RADIX), :] = o[c * RADIX : (c + 1) * RADIX]
            if rows > 2 * RADIX:
                spec[c, pl.ds(RADIX - k1, RADIX, stride=RADIX), :] = o[
                    (2 + c) * RADIX : (3 + c) * RADIX
                ]

    second(0, 2 * RADIX)
    second(HALF, 2 * RADIX)

    @pl.loop(1, HALF)
    def _(k1):
        second(k1, 4 * RADIX)

    @pl.loop(0, groups)
    def _(g):
        for c in range(2):
            start = g * group
            for ref in out_refs:
                size = ref.shape[2]
                ref[g, c] = spec[c, pl.ds(pl.multiple_of(start, size), size), :].astype(jnp.bfloat16)
                start = start + size


def spectrum_of(old, mid, new, taps, groups, pieces):
    inputs = new[0].shape[0]
    length = taps.shape[1]
    assert length == RADIX * LANES and inputs == LANES and taps.shape[0] == 3
    channels = length // 2
    size = channels // groups // pieces
    twist, table = dft_tables(length)

    def block(index):
        return pl.BlockSpec((inputs, length), lambda i: (0, index))

    def whole(array):
        return pl.BlockSpec(array.shape, lambda i: (0,) * array.ndim)

    out = jax.ShapeDtypeStruct((groups, 2, size, inputs), jnp.bfloat16)
    return pl.pallas_call(
        fft_kernel,
        grid=(1,),
        out_shape=[out] * pieces,
        in_specs=[block(old[1]), block(mid[1]), block(new[1]), whole(taps), whole(twist), whole(table)],
        out_specs=[whole(out)] * pieces,
        scratch_shapes=[
            pltpu.VMEM((HALF + 1, inputs, 2 * LANES), jnp.bfloat16),
            pltpu.VMEM((HALF + 1, inputs, 2 * LANES), jnp.bfloat16),
            pltpu.VMEM((2, channels, inputs), jnp.float32),
        ],
        compiler_params=pltpu.CompilerParams(vmem_limit_bytes=VMEM_BYTES),
        cost_estimate=pl.CostEstimate(
            flops=12_000_000_000, bytes_accessed=8_000_000, transcendentals=0
        ),
    )(old[0], mid[0], new[0], taps, jnp.asarray(twist), jnp.asarray(table))


def pair_kernel(scale, pair_ref, late_ref, early_ref, pick_ref, *rest):
    out_ref, turned_left, turned_right, gram = rest[-4:]
    depth, chunk, inputs = late_ref.shape
    rows = depth * chunk
    depth = 2 * depth
    pairs = pair_ref.shape[0]
    half = depth // 2
    for i, ref in enumerate((late_ref, early_ref)):
        data = ref[...].reshape(rows, inputs)
        for side, turned in enumerate((turned_left, turned_right)):
            turned[i * rows : (i + 1) * rows, :] = jnp.dot(
                data, pick_ref[side], preferred_element_type=jnp.float32
            )
    lane_group = lax.broadcasted_iota(jnp.int32, (8, LANES), 1) // BLOCK_SIZE
    masks = [lane_group == j for j in range(4)]
    firsts = [pl.multiple_of(pair_ref[p, 0] * BLOCK_SIZE, BLOCK_SIZE) for p in range(pairs)]
    shifts = [
        [lax.rem(j - pair_ref[p, 1] + 4, 4) * BLOCK_SIZE for j in range(4)] for p in range(pairs)
    ]
    dims = (((0,), (0,)), ((), ()))
    unroll = gram.shape[0]

    @pl.loop(0, chunk // unroll)
    def _(step):
        for i in range(unroll):
            ch = step * unroll + i

            def operand(ref):
                re = ref[pl.ds(ch, half, stride=2 * chunk), :]
                im = ref[pl.ds(chunk + ch, half, stride=2 * chunk), :]
                return re, im

            re, im = operand(turned_left)
            left = jnp.concatenate([re, im], 0).astype(jnp.bfloat16)
            re, im = operand(turned_right)
            re, im = re * scale, im * scale
            right = jnp.concatenate(
                [jnp.concatenate([re, im], 0), jnp.concatenate([-im, re], 0)], 1
            ).astype(jnp.bfloat16)
            gram[i] = lax.dot_general(left, right, dims, preferred_element_type=jnp.float32)
        for i in range(unroll):
            ch = step * unroll + i
            for c in range(2):
                for p in range(pairs):
                    tile = None
                    for j in range(4):
                        piece = gram[
                            i, pl.ds(firsts[p] + 8 * j, 8), c * LANES : (c + 1) * LANES
                        ]
                        piece = pltpu.roll(piece, shifts[p][j], 1)
                        tile = piece if tile is None else jnp.where(masks[j], piece, tile)
                    out_ref[c, ch, pl.ds(p, 8, stride=pairs), :] = tile


def visibilities_of(late, early, base, pick, pair_list, scale, channels, earlier):
    depth, size, inputs = early.shape
    pairs = pair_list.shape[0]
    chunk = min(32, size)
    first = base // chunk
    operands = [pair_list, late, early, pick]
    in_specs = [
        pl.BlockSpec((depth, chunk, inputs), lambda i, _: (0, first + i, 0)),
        pl.BlockSpec((depth, chunk, inputs), lambda i, _: (0, i, 0)),
        pl.BlockSpec((2, inputs, inputs), lambda i, _: (0, 0, 0)),
    ]
    aliases = {}
    if earlier is not None:
        aliases = {len(operands): 0}
        operands.append(earlier)
        in_specs.append(pl.BlockSpec(memory_space=pl.ANY))
    return pl.pallas_call(
        functools.partial(pair_kernel, scale),
        grid_spec=pltpu.PrefetchScalarGridSpec(
            num_scalar_prefetch=1,
            grid=(size // chunk,),
            in_specs=in_specs,
            out_specs=pl.BlockSpec(
                (2, chunk, 8 * pairs, LANES), lambda i, _: (0, first + i, 0, 0)
            ),
            scratch_shapes=[
                pltpu.VMEM((2 * depth * chunk, inputs), jnp.float32),
                pltpu.VMEM((2 * depth * chunk, inputs), jnp.float32),
                pltpu.VMEM((min(UNROLL, chunk), inputs, 2 * inputs), jnp.float32),
            ],
        ),
        out_shape=jax.ShapeDtypeStruct((2, channels, 8 * pairs, LANES), jnp.float32),
        input_output_aliases=aliases,
        compiler_params=pltpu.CompilerParams(
            vmem_limit_bytes=VMEM_BYTES, dimension_semantics=("arbitrary",)
        ),
        cost_estimate=pl.CostEstimate(
            flops=20_000_000_000 // (channels // size), bytes_accessed=20_000_000, transcendentals=0
        ),
    )(*operands)


def input_order(station_order):
    return (2 * station_order[:, None] + jnp.arange(2, dtype=jnp.int32)[None, :]).reshape(-1)


def shards(row_count, voltages, taps, station_order, pair_list):
    order = input_order(station_order)
    inputs = voltages.shape[0]
    left_order = jnp.swapaxes(order.reshape(-1, BLOCK_SIZE // 4, 4), 1, 2).reshape(-1)
    both = jnp.stack([left_order, order])
    pick = (jnp.arange(inputs, dtype=jnp.int32)[None, :, None] == both[:, None, :]).astype(jnp.bfloat16)
    length = taps.shape[1]
    assert voltages.shape[1] == 2 * length
    onward = [(i, i + 1) for i in range(row_count - 1)]
    past_two = lax.ppermute(voltages[:, length:], "row", onward)
    sent, past_two = lax.optimization_barrier((voltages[:, :length], past_two))
    past_one = lax.ppermute(sent, "row", onward)
    channels = length // 2 // row_count

    def exchange(piece):
        moved = lax.all_to_all(piece, "row", split_axis=0, concat_axis=0, tiled=True)
        return moved.reshape(2 * row_count, piece.shape[2], inputs)

    (second,) = spectrum_of((past_two, 0), (voltages, 0), (voltages, 1), taps, row_count, 1)
    late = exchange(second)
    firsts = spectrum_of((past_one, 0), (past_two, 0), (voltages, 0), taps, row_count, PIECES)
    result = None
    for index, piece in enumerate(firsts):
        early = exchange(piece)
        base = index * early.shape[1]
        result = visibilities_of(
            late, early, base, pick, pair_list, 1.0 / (2 * row_count), channels, result
        )
    pairs = pair_list.shape[0]
    tiles = result.reshape(2, channels, 8, pairs, LANES)
    return jnp.swapaxes(tiles, 2, 3).reshape(2, channels, pairs, BLOCK_SIZE * BLOCK_SIZE)


def solution(mesh):
    placed = (P("grp", "row"), P(), P("grp"), P("grp", None))
    return jax.shard_map(
        functools.partial(shards, mesh.shape["row"]),
        mesh=mesh,
        in_specs=placed,
        out_specs=P(None, "row", "grp", None),
        check_vma=False,
    )
```

time: 290 us -> 231 us (0.80)
  Pallas kernels: 138 us -> 81.3 us
  waiting for transfers between devices: 137 us -> 89.4 us
  blocking collectives: 0 us -> 31.2 us
  starting transfers between devices: 11 us -> 19.3 us
  local copies, waits for them, and re-layouts: 2.83 us -> 8.81 us
    all_to_all x1 -> x2, waiting for transfers between devices: 90.9 us -> 1.49 us  [exchange(): lax.all_to_all(piece, 'row', split_axis=0, concat_axis=0, tiled=True)]
    pallas_call x1 -> x2, Pallas kernels: 103 us -> 42.7 us  [visibilities_of(): pl.pallas_call(functools.partial(pair_kernel, scale), grid_spec=pltpu.Pre...]
    ppermute x1 -> x2, waiting for transfers between devices: 45.7 us -> 87.9 us  [the longest x1 65 us: shards(): past_one = lax.ppermute(sent, 'row', onward)]
    all_to_all x0 -> x1, blocking collectives: none -> 31.2 us  [exchange(): lax.all_to_all(piece, 'row', split_axis=0, concat_axis=0, tiled=True)]
    all_to_all x1 -> x2, starting transfers between devices: 7.23 us -> 12.3 us  [exchange(): lax.all_to_all(piece, 'row', split_axis=0, concat_axis=0, tiled=True)]
    slice x0 -> x1, local copies, waits for them, and re-layouts: none -> 3.98 us  [shards(): past_two = lax.ppermute(voltages[:, length:], 'row', onward)]
    ppermute x1 -> x2, starting transfers between devices: 3.72 us -> 7.05 us  [the longest x1 3.72 us: shards(): past_two = lax.ppermute(voltages[:, length:], 'row', onward)]
    pallas_call x1 -> x2, Pallas kernels: 35.7 us -> 38.6 us  [spectrum_of(): pl.pallas_call(fft_kernel, grid=(1,), out_shape=[out] * pieces, in_specs=...]
  transfers between devices with their start and end apart: 2 -> 4, of which waited for: 2 -> 3; matrix products, arithmetic and copies ran while one was open for 1% -> 1% of each run, Pallas kernels for 0% -> 18%
where the time goes in v2:
time: 231 us
  waiting for transfers between devices  89.4 us (39%)
  Pallas kernels  81.3 us (35%)
  blocking collectives  31.2 us (14%)
  starting transfers between devices  19.3 us (8%)
  local copies, waits for them, and re-layouts  8.81 us (4%)
    ppermute x1, waiting for transfers between devices, shards(): past_one = lax.ppermute(sent, 'row', onward)  65 us
    pallas_call x2, Pallas kernels, visibilities_of(): pl.pallas_call(functools.partial(pair_kernel, scale), grid_spec=pltpu.Pre...  42.7 us
    pallas_call x2, Pallas kernels, spectrum_of(): pl.pallas_call(fft_kernel, grid=(1,), out_shape=[out] * pieces, in_specs=...  38.6 us
    all_to_all x1, blocking collectives, exchange(): lax.all_to_all(piece, 'row', split_axis=0, concat_axis=0, tiled=True)  31.2 us
    ppermute x1, waiting for transfers between devices, shards(): past_two = lax.ppermute(voltages[:, length:], 'row', onward)  23 us
    all_to_all x2, starting transfers between devices, exchange(): lax.all_to_all(piece, 'row', split_axis=0, concat_axis=0, tiled=True)  12.3 us
  transfers between devices with their start and end apart: 4, of which 3 were waited for; matrix products, arithmetic and copies ran while one was open for 1% of the time, Pallas kernels for 18%

profile of v2, /device:TPU:11, one launch (start us, length us, event | category | flops | bytes accessed | tf_op | source)
XLA Modules:
  0.0 231.0 jit_solution(17860707494664102216)
XLA Ops:
  0.0 4.0 %fusion.1 = (bf16[128,8192]{1,0:T(8,128)(2,1)S(1)}, bf16[128,8192]{1,0:T(8,128)(2,1)}) fusion(bf16[128,16384]{1,0:T(8,128)(2,1)} %new_ref.3), kind=kLoop, calls=%fused_computation.6 | loop fusion | bytes 8388608 | tf_op jit(solution)/shard_map/slice | solution.py:324
  4.0 3.7 %collective-permute-start = (bf16[128,8192]{1,0:T(8,128)(2,1)S(1)}, bf16[128,8192]{1,0:T(8,128)(2,1)S(1)}, u32[]{:S(2)}, u32[]{:S(2)}) collective-permute-start(bf16[128,8192]{1,0:T(8,128)(2,1)S(1)} %get-tuple-element.13), channel_id=1, source_target_pairs={{0,1},{1,2},{2,3},{3,4},{4,5},{5,6},{6,7},{7,8},{8,9},{9,10},{10,1... | collective-permute-start | bytes 6291464 | tf_op jit(solution)/shard_map/ppermute | solution.py:324
  7.7 23.0 %collective-permute-done.old_ref.mid_ref = bf16[128,8192]{1,0:T(8,128)(2,1)S(1)} collective-permute-done((bf16[128,8192]{1,0:T(8,128)(2,1)S(1)}, bf16[128,8192]{1,0:T(8,128)(2,1)S(1)}, u32[]{:S(2)}, u32[]{:S(2)}) %collective-permute-start) | collective-permute-done | bytes 2097184 | tf_op jit(solution)/shard_map/ppermute | solution.py:324
  30.7 0.0 copy-start.3
  30.7 1.3 copy-done.3
  32.0 19.3 %shard_map.82 = bf16[16,2,256,128]{3,2,1,0:T(8,128)(2,1)} custom-call(bf16[128,8192]{1,0:T(8,128)(2,1)} %copy-done.3, bf16[128,16384]{1,0:T(8,128)(2,1)} %new_ref.3, bf16[128,16384]{1,0:T(8,128)(2,1)} %new_ref.3, f32[3,8192]{1,0:T(4,128)} %taps_ref.3, f32[2,33,128]{2,1,0:T(8,128)} %constant.6.clone.twist_ref, bf16[2,256,256]{2,1,0:T(8,128)(2,1)} %constant.7.clone.table_ref), custom_call_target="tpu_custom_call" | custom-call | flops 12000000000 | bytes 8000000 | tf_op jit(solution)/shard_map/pallas_call | solution.py:197
  51.3 7.2 %all-to-all-start = ((bf16[16,2,256,128]{3,2,1,0:T(8,128)(2,1)}), bf16[16,2,256,128]{3,2,1,0:T(8,128)(2,1)S(1)}, u32[]{:S(2)}, u32[]{:S(2)}) async-start(bf16[16,2,256,128]{3,2,1,0:T(8,128)(2,1)} %shard_map.82), calls=%async_computation | async-start | bytes 4194304 | tf_op jit(solution)/shard_map/all_to_all | solution.py:330
  58.6 3.3 %collective-permute-start.1 = (bf16[128,8192]{1,0:T(8,128)(2,1)}, bf16[128,8192]{1,0:T(8,128)(2,1)S(1)}, u32[]{:S(2)}, u32[]{:S(2)}) collective-permute-start(bf16[128,8192]{1,0:T(8,128)(2,1)} %get-tuple-element.10), channel_id=1, source_target_pairs={{0,1},{1,2},{2,3},{3,4},{4,5},{5,6},{6,7},{7,8},{8,9},{9,10},{10,1... | collective-permute-start | bytes 6291464 | tf_op jit(solution)/shard_map/ppermute | solution.py:326
  61.9 65.0 %collective-permute-done.1.old_ref = bf16[128,8192]{1,0:T(8,128)(2,1)S(1)} collective-permute-done((bf16[128,8192]{1,0:T(8,128)(2,1)}, bf16[128,8192]{1,0:T(8,128)(2,1)S(1)}, u32[]{:S(2)}, u32[]{:S(2)}) %collective-permute-start.1) | collective-permute-done | bytes 2097184 | tf_op jit(solution)/shard_map/ppermute | solution.py:326
  126.9 0.0 copy-start.4
  126.9 1.3 copy-done.4
  128.2 19.3 %shard_map.83 = (bf16[16,2,128,128]{3,2,1,0:T(8,128)(2,1)}, bf16[16,2,128,128]{3,2,1,0:T(8,128)(2,1)}) custom-call(bf16[128,8192]{1,0:T(8,128)(2,1)} %copy-done.4, bf16[128,8192]{1,0:T(8,128)(2,1)} %copy-done.3, bf16[128,16384]{1,0:T(8,128)(2,1)} %new_ref.3, f32[3,8192]{1,0:T(4,128)} %taps_ref.3, f32[2,33,128]{2,1,0:T(8,128)} %constant.6.clone.twist_ref, ...), custom_call_target="tpu_custom_call" | custom-call | flops 12000000000 | bytes 8000000 | tf_op jit(solution)/shard_map/pallas_call | solution.py:197
  147.5 0.0 all-to-all-done
  147.5 0.0 copy-start.5
  147.5 31.2 %all_to_all.15 = bf16[16,2,128,128]{3,2,1,0:T(8,128)(2,1)} all-to-all(bf16[16,2,128,128]{3,2,1,0:T(8,128)(2,1)} %get-tuple-element.12), channel_id=1, replica_groups=mesh['grp'=2,'row'=16] {'row'}, dimensions={0} | all-to-all | bytes 2097152 | tf_op jit(solution)/shard_map/all_to_all | solution.py:330
  178.7 0.0 copy-done
  178.7 5.0 %all-to-all-start.1 = ((bf16[16,2,128,128]{3,2,1,0:T(8,128)(2,1)}), bf16[16,2,128,128]{3,2,1,0:T(8,128)(2,1)S(1)}, u32[]{:S(2)}, u32[]{:S(2)}) async-start(bf16[16,2,128,128]{3,2,1,0:T(8,128)(2,1)} %get-tuple-element.11), calls=%async_computation.1 | async-start | bytes 2097152 | tf_op jit(solution)/shard_map/all_to_all | solution.py:330
  183.8 0.1 add.42
  183.8 0.0 copy-done.2
  183.8 0.7 copy.15.pair_ref
  184.5 0.0 copy-done.5
  184.5 0.1 add.38
  184.6 0.1 copy.13
  184.7 0.1 add_bitcast_fusion
  184.8 0.1 stack_reshape.4
  184.9 0.1 iota_add_fusion
  185.0 0.1 add.48
  185.2 0.6 fusion.pick_ref
  185.8 21.4 %shard_map.84.rest_0_ = f32[2,256,64,128]{3,2,1,0:T(8,128)} custom-call(s32[8,2]{1,0:T(8,128)} %copy.15.pair_ref, bf16[32,256,128]{2,1,0:T(8,128)(2,1)} %bitcast.11, bf16[32,128,128]{2,1,0:T(8,128)(2,1)} %bitcast.14, bf16[2,128,128]{2,1,0:T(8,128)(2,1)} %fusion.pick_ref), custom_call_target="tpu_custom_call" | custom-call | flops 10000000000 | bytes 20000000 | tf_op jit(solution)/shard_map/pallas_call | solution.py:285
  207.1 1.5 all-to-all-done.1
  208.6 1.0 copy-done.1
  209.6 21.4 %shard_map.85 = f32[2,256,64,128]{3,2,1,0:T(8,128)} custom-call(s32[8,2]{1,0:T(8,128)} %copy.15.pair_ref, bf16[32,256,128]{2,1,0:T(8,128)(2,1)} %bitcast.12, bf16[32,128,128]{2,1,0:T(8,128)(2,1)} %bitcast.13, bf16[2,128,128]{2,1,0:T(8,128)(2,1)} %fusion.pick_ref, f32[2,256,64,128]{3,2,1,0:T(8,128)} %shard_map.84.rest_0_), custom_call_target="tpu_custom_call", output_to_operand_aliasing={{}: (4, {})} | custom-call | flops 10000000000 | bytes 20000000 | tf_op jit(solution)/shard_map/pallas_call | solution.py:285
  (7 shorter events, 0.0 us)
Async XLA Ops:
  4.0 26.7 %collective-permute-start = (bf16[128,8192]{1,0:T(8,128)(2,1)S(1)}, bf16[128,8192]{1,0:T(8,128)(2,1)S(1)}, u32[]{:S(2)}, u32[]{:S(2)}) collective-permute-start(bf16[128,8192]{1,0:T(8,128)(2,1)S(1)} %get-tuple-element.13), channel_id=1, source_target_pairs={{0,1},{1,2},{2,3},{3,4},{4,5},{5,6},{6,7},{7,8},{8,9},{9,10},{10,1... | collective-permute-start | bytes 6291464 | tf_op jit(solution)/shard_map/ppermute | solution.py:324
  30.7 1.3 copy-start.3
  51.3 96.2 %all-to-all-start = ((bf16[16,2,256,128]{3,2,1,0:T(8,128)(2,1)}), bf16[16,2,256,128]{3,2,1,0:T(8,128)(2,1)S(1)}, u32[]{:S(2)}, u32[]{:S(2)}) async-start(bf16[16,2,256,128]{3,2,1,0:T(8,128)(2,1)} %shard_map.82), calls=%async_computation | async-start | bytes 4194304 | tf_op jit(solution)/shard_map/all_to_all | solution.py:330
  58.6 68.3 %collective-permute-start.1 = (bf16[128,8192]{1,0:T(8,128)(2,1)}, bf16[128,8192]{1,0:T(8,128)(2,1)S(1)}, u32[]{:S(2)}, u32[]{:S(2)}) collective-permute-start(bf16[128,8192]{1,0:T(8,128)(2,1)} %get-tuple-element.10), channel_id=1, source_target_pairs={{0,1},{1,2},{2,3},{3,4},{4,5},{5,6},{6,7},{7,8},{8,9},{9,10},{10,1... | collective-permute-start | bytes 6291464 | tf_op jit(solution)/shard_map/ppermute | solution.py:326
  126.9 1.3 copy-start.4
  147.5 31.2 %copy-start = (bf16[16,2,256,128]{3,2,1,0:T(8,128)(2,1)}, bf16[16,2,256,128]{3,2,1,0:T(8,128)(2,1)S(1)}, u32[]{:S(2)}) copy-start(bf16[16,2,256,128]{3,2,1,0:T(8,128)(2,1)S(1)} %all-to-all-done) | copy-start | bytes 6291460
  147.5 36.3 %copy-start.2 = (s32[8,2]{0,1:T(2,128)S(1)}, s32[8,2]{0,1:T(2,128)}, u32[]{:S(2)}) copy-start(s32[8,2]{0,1:T(2,128)} %param.11) | copy-start | bytes 196
  147.5 37.0 %copy-start.5 = (s32[64]{0:T(128)S(1)}, s32[64]{0:T(128)}, u32[]{:S(2)}) copy-start(s32[64]{0:T(128)} %param.10) | copy-start | bytes 772
  178.7 29.9 %all-to-all-start.1 = ((bf16[16,2,128,128]{3,2,1,0:T(8,128)(2,1)}), bf16[16,2,128,128]{3,2,1,0:T(8,128)(2,1)S(1)}, u32[]{:S(2)}, u32[]{:S(2)}) async-start(bf16[16,2,128,128]{3,2,1,0:T(8,128)(2,1)} %get-tuple-element.11), calls=%async_computation.1 | async-start | bytes 2097152 | tf_op jit(solution)/shard_map/all_to_all | solution.py:330
  208.6 1.0 copy-start.1

commit v3 on v2

--- a/solution.py
+++ b/solution.py
@@ -325,14 +325,16 @@
     sent, past_two = lax.optimization_barrier((voltages[:, :length], past_two))
     past_one = lax.ppermute(sent, "row", onward)
     channels = length // 2 // row_count
+    pieces = min(PIECES, channels // 16)
 
     def exchange(piece):
         moved = lax.all_to_all(piece, "row", split_axis=0, concat_axis=0, tiled=True)
         return moved.reshape(2 * row_count, piece.shape[2], inputs)
 
     (second,) = spectrum_of((past_two, 0), (voltages, 0), (voltages, 1), taps, row_count, 1)
+    second, past_one = lax.optimization_barrier((second, past_one))
     late = exchange(second)
-    firsts = spectrum_of((past_one, 0), (past_two, 0), (voltages, 0), taps, row_count, PIECES)
+    firsts = spectrum_of((past_one, 0), (past_two, 0), (voltages, 0), taps, row_count, pieces)
     result = None
     for index, piece in enumerate(firsts):
         early = exchange(piece)

time: 231 us -> 216 us (0.935)
  waiting for transfers between devices: 89.4 us -> 28 us
  blocking collectives: 31.2 us -> 84.5 us
  starting transfers between devices: 19.3 us -> 14.3 us
  local copies, waits for them, and re-layouts: 8.81 us -> 6.17 us
    ppermute x1, waiting for transfers between devices: 65 us -> 3.6 us  [shards(): past_one = lax.ppermute(sent, 'row', onward)]
    all_to_all x1 -> x2, blocking collectives: 31.2 us -> 84.5 us  [exchange(): lax.all_to_all(piece, 'row', split_axis=0, concat_axis=0, tiled=True)]
    all_to_all x2 -> x1, starting transfers between devices: 12.3 us -> 5.25 us  [exchange(): lax.all_to_all(piece, 'row', split_axis=0, concat_axis=0, tiled=True)]
  transfers between devices with their start and end apart: 4 -> 3, of which waited for: 3 -> 3; matrix products, arithmetic and copies ran while one was open for 1% -> 1% of each run, Pallas kernels for 18% -> 19%
where the time goes in v3:
time: 216 us; the launch traced here: 215 us
  blocking collectives  84.5 us (39%)
  Pallas kernels  81.4 us (38%)
  waiting for transfers between devices  28 us (13%)
  starting transfers between devices  14.3 us (7%)
  local copies, waits for them, and re-layouts  6.17 us (3%)
    all_to_all x2, blocking collectives, exchange(): lax.all_to_all(piece, 'row', split_axis=0, concat_axis=0, tiled=True)  84.5 us
    pallas_call x2, Pallas kernels, visibilities_of(): pl.pallas_call(functools.partial(pair_kernel, scale), grid_spec=pltpu.Pre...  42.7 us
    pallas_call x2, Pallas kernels, spectrum_of(): pl.pallas_call(fft_kernel, grid=(1,), out_shape=[out] * pieces, in_specs=...  38.6 us
    ppermute x1, waiting for transfers between devices, shards(): past_two = lax.ppermute(voltages[:, length:], 'row', onward)  23 us
    ppermute x1, starting transfers between devices, shards(): past_one = lax.ppermute(sent, 'row', onward)  5.28 us
    all_to_all x1, starting transfers between devices, exchange(): lax.all_to_all(piece, 'row', split_axis=0, concat_axis=0, tiled=True)  5.25 us
  transfers between devices with their start and end apart: 3, of which 3 were waited for; matrix products, arithmetic and copies ran while one was open for 1% of the time, Pallas kernels for 19%

profile of v3, /device:TPU:11, one launch (start us, length us, event | category | flops | bytes accessed | tf_op | source)
XLA Modules:
  0.0 215.2 jit_solution(13402724015204003081)
XLA Ops:
  0.0 2.6 %fusion.1 = (bf16[128,8192]{1,0:T(8,128)(2,1)S(1)}, bf16[128,8192]{1,0:T(8,128)(2,1)S(1)}) fusion(bf16[128,16384]{1,0:T(8,128)(2,1)} %new_ref.3), kind=kLoop, calls=%fused_computation.6 | loop fusion | bytes 8388608 | tf_op jit(solution)/shard_map/slice | solution.py:324
  2.7 3.7 %collective-permute-start = (bf16[128,8192]{1,0:T(8,128)(2,1)S(1)}, bf16[128,8192]{1,0:T(8,128)(2,1)S(1)}, u32[]{:S(2)}, u32[]{:S(2)}) collective-permute-start(bf16[128,8192]{1,0:T(8,128)(2,1)S(1)} %get-tuple-element.17), channel_id=1, source_target_pairs={{0,1},{1,2},{2,3},{3,4},{4,5},{5,6},{6,7},{7,8},{8,9},{9,10},{10,1... | collective-permute-start | bytes 6291464 | tf_op jit(solution)/shard_map/ppermute | solution.py:324
  6.4 23.0 %collective-permute-done.old_ref.mid_ref = bf16[128,8192]{1,0:T(8,128)(2,1)S(1)} collective-permute-done((bf16[128,8192]{1,0:T(8,128)(2,1)S(1)}, bf16[128,8192]{1,0:T(8,128)(2,1)S(1)}, u32[]{:S(2)}, u32[]{:S(2)}) %collective-permute-start) | collective-permute-done | bytes 2097184 | tf_op jit(solution)/shard_map/ppermute | solution.py:324
  29.4 0.0 copy-start.3
  29.4 5.3 %collective-permute-start.1 = (bf16[128,8192]{1,0:T(8,128)(2,1)S(1)}, bf16[128,8192]{1,0:T(8,128)(2,1)S(1)}, u32[]{:S(2)}, u32[]{:S(2)}) collective-permute-start(bf16[128,8192]{1,0:T(8,128)(2,1)S(1)} %get-tuple-element.12), channel_id=1, source_target_pairs={{0,1},{1,2},{2,3},{3,4},{4,5},{5,6},{6,7},{7,8},{8,9},{9,10},{10,1... | collective-permute-start | bytes 6291464 | tf_op jit(solution)/shard_map/ppermute | solution.py:326
  34.6 0.0 copy-done.3
  34.7 19.4 %shard_map.82 = bf16[16,2,256,128]{3,2,1,0:T(8,128)(2,1)} custom-call(bf16[128,8192]{1,0:T(8,128)(2,1)} %copy-done.3, bf16[128,16384]{1,0:T(8,128)(2,1)} %new_ref.3, bf16[128,16384]{1,0:T(8,128)(2,1)} %new_ref.3, f32[3,8192]{1,0:T(4,128)} %taps_ref.3, f32[2,33,128]{2,1,0:T(8,128)} %constant.6.clone.twist_ref, bf16[2,256,256]{2,1,0:T(8,128)(2,1)} %constant.7.clone.table_ref), custom_call_target="tpu_custom_call" | custom-call | flops 12000000000 | bytes 8000000 | tf_op jit(solution)/shard_map/pallas_call | solution.py:197
  54.0 3.6 %collective-permute-done.1.old_ref = bf16[128,8192]{1,0:T(8,128)(2,1)S(1)} collective-permute-done((bf16[128,8192]{1,0:T(8,128)(2,1)S(1)}, bf16[128,8192]{1,0:T(8,128)(2,1)S(1)}, u32[]{:S(2)}, u32[]{:S(2)}) %collective-permute-start.1) | collective-permute-done | bytes 2097184 | tf_op jit(solution)/shard_map/ppermute | solution.py:326
  57.6 0.0 copy-start.4
  57.6 1.3 copy-done.4
  58.9 19.3 %shard_map.83 = (bf16[16,2,128,128]{3,2,1,0:T(8,128)(2,1)}, bf16[16,2,128,128]{3,2,1,0:T(8,128)(2,1)}) custom-call(bf16[128,8192]{1,0:T(8,128)(2,1)} %copy-done.4, bf16[128,8192]{1,0:T(8,128)(2,1)} %copy-done.3, bf16[128,16384]{1,0:T(8,128)(2,1)} %new_ref.3, f32[3,8192]{1,0:T(4,128)} %taps_ref.3, f32[2,33,128]{2,1,0:T(8,128)} %constant.6.clone.twist_ref, ...), custom_call_target="tpu_custom_call" | custom-call | flops 12000000000 | bytes 8000000 | tf_op jit(solution)/shard_map/pallas_call | solution.py:197
  78.2 0.0 copy-start
  78.2 32.2 %all_to_all.15 = bf16[16,2,128,128]{3,2,1,0:T(8,128)(2,1)} all-to-all(bf16[16,2,128,128]{3,2,1,0:T(8,128)(2,1)} %get-tuple-element.16), channel_id=1, replica_groups=mesh['grp'=2,'row'=16] {'row'}, dimensions={0} | all-to-all | bytes 2097152 | tf_op jit(solution)/shard_map/all_to_all | solution.py:331
  110.5 0.0 copy-done
  110.5 52.2 %all_to_all.16 = bf16[16,2,256,128]{3,2,1,0:T(8,128)(2,1)} all-to-all(bf16[16,2,256,128]{3,2,1,0:T(8,128)(2,1)S(1)} %copy-done), channel_id=1, replica_groups=mesh['grp'=2,'row'=16] {'row'}, dimensions={0} | all-to-all | bytes 4194304 | tf_op jit(solution)/shard_map/all_to_all | solution.py:331
  162.7 0.0 copy-start.2
  162.7 5.3 %all-to-all-start.1 = ((bf16[16,2,128,128]{3,2,1,0:T(8,128)(2,1)}), bf16[16,2,128,128]{3,2,1,0:T(8,128)(2,1)S(1)}, u32[]{:S(2)}, u32[]{:S(2)}) async-start(bf16[16,2,128,128]{3,2,1,0:T(8,128)(2,1)} %get-tuple-element.15), calls=%async_computation.1 | async-start | bytes 2097152 | tf_op jit(solution)/shard_map/all_to_all | solution.py:331
  167.9 0.1 add.42
  168.0 0.0 copy-done.2
  168.0 0.7 copy.15.pair_ref
  168.7 0.0 copy-done.5
  168.7 0.1 add.38
  168.8 0.1 copy.13
  168.9 0.1 add_bitcast_fusion
  169.0 0.1 stack_reshape.4
  169.1 0.1 iota_add_fusion
  169.2 0.1 add.48
  169.3 0.6 fusion.pick_ref
  170.0 21.3 %shard_map.84.rest_0_ = f32[2,256,64,128]{3,2,1,0:T(8,128)} custom-call(s32[8,2]{1,0:T(8,128)} %copy.15.pair_ref, bf16[32,256,128]{2,1,0:T(8,128)(2,1)} %bitcast.11, bf16[32,128,128]{2,1,0:T(8,128)(2,1)} %bitcast.14, bf16[2,128,128]{2,1,0:T(8,128)(2,1)} %fusion.pick_ref), custom_call_target="tpu_custom_call" | custom-call | flops 10000000000 | bytes 20000000 | tf_op jit(solution)/shard_map/pallas_call | solution.py:285
  191.3 1.5 all-to-all-done.1
  192.8 1.0 copy-done.1
  193.8 21.4 %shard_map.85 = f32[2,256,64,128]{3,2,1,0:T(8,128)} custom-call(s32[8,2]{1,0:T(8,128)} %copy.15.pair_ref, bf16[32,256,128]{2,1,0:T(8,128)(2,1)} %bitcast.12, bf16[32,128,128]{2,1,0:T(8,128)(2,1)} %bitcast.13, bf16[2,128,128]{2,1,0:T(8,128)(2,1)} %fusion.pick_ref, f32[2,256,64,128]{3,2,1,0:T(8,128)} %shard_map.84.rest_0_), custom_call_target="tpu_custom_call", output_to_operand_aliasing={{}: (4, {})} | custom-call | flops 10000000000 | bytes 20000000 | tf_op jit(solution)/shard_map/pallas_call | solution.py:285
  (6 shorter events, 0.0 us)
Async XLA Ops:
  2.7 26.7 %collective-permute-start = (bf16[128,8192]{1,0:T(8,128)(2,1)S(1)}, bf16[128,8192]{1,0:T(8,128)(2,1)S(1)}, u32[]{:S(2)}, u32[]{:S(2)}) collective-permute-start(bf16[128,8192]{1,0:T(8,128)(2,1)S(1)} %get-tuple-element.17), channel_id=1, source_target_pairs={{0,1},{1,2},{2,3},{3,4},{4,5},{5,6},{6,7},{7,8},{8,9},{9,10},{10,1... | collective-permute-start | bytes 6291464 | tf_op jit(solution)/shard_map/ppermute | solution.py:324
  29.4 5.3 %copy-start.3 = (bf16[128,8192]{1,0:T(8,128)(2,1)}, bf16[128,8192]{1,0:T(8,128)(2,1)S(1)}, u32[]{:S(2)}) copy-start(bf16[128,8192]{1,0:T(8,128)(2,1)S(1)} %collective-permute-done.old_ref.mid_ref) | copy-start | bytes 6291460
  29.4 28.2 %collective-permute-start.1 = (bf16[128,8192]{1,0:T(8,128)(2,1)S(1)}, bf16[128,8192]{1,0:T(8,128)(2,1)S(1)}, u32[]{:S(2)}, u32[]{:S(2)}) collective-permute-start(bf16[128,8192]{1,0:T(8,128)(2,1)S(1)} %get-tuple-element.12), channel_id=1, source_target_pairs={{0,1},{1,2},{2,3},{3,4},{4,5},{5,6},{6,7},{7,8},{8,9},{9,10},{10,1... | collective-permute-start | bytes 6291464 | tf_op jit(solution)/shard_map/ppermute | solution.py:326
  57.6 1.3 copy-start.4
  78.2 32.3 %copy-start = (bf16[16,2,256,128]{3,2,1,0:T(8,128)(2,1)S(1)}, bf16[16,2,256,128]{3,2,1,0:T(8,128)(2,1)}, u32[]{:S(2)}) copy-start(bf16[16,2,256,128]{3,2,1,0:T(8,128)(2,1)} %shard_map.82) | copy-start | bytes 6291460
  162.7 5.3 %copy-start.2 = (s32[8,2]{0,1:T(2,128)S(1)}, s32[8,2]{0,1:T(2,128)}, u32[]{:S(2)}) copy-start(s32[8,2]{0,1:T(2,128)} %param.11) | copy-start | bytes 196
  162.7 6.0 %copy-start.5 = (s32[64]{0:T(128)S(1)}, s32[64]{0:T(128)}, u32[]{:S(2)}) copy-start(s32[64]{0:T(128)} %param.10) | copy-start | bytes 772
  162.7 30.1 %all-to-all-start.1 = ((bf16[16,2,128,128]{3,2,1,0:T(8,128)(2,1)}), bf16[16,2,128,128]{3,2,1,0:T(8,128)(2,1)S(1)}, u32[]{:S(2)}, u32[]{:S(2)}) async-start(bf16[16,2,128,128]{3,2,1,0:T(8,128)(2,1)} %get-tuple-element.15), calls=%async_computation.1 | async-start | bytes 2097152 | tf_op jit(solution)/shard_map/all_to_all | solution.py:331
  192.8 1.0 copy-start.1
